TPU v7x, 256 devices: a whole 4x4x8 slice. The times are simulated.
256 devices in a mesh: grp: 4 (over z_hi, core), dev: 64 (over z_lo, y, x).
Axes of the slice: x: 4, y: 4, z: 8 (z_hi: 2, z_lo: 4; z = z_hi * 4 + z_lo), core: 2. Of those that a mesh axis runs over, the one named last changes fastest.
Arguments:
- key_tokens: bfloat16 [32768, 768], P(('grp', 'dev')), may hold values from -6 to 6
- value_tokens: bfloat16 [32768, 768], P(('grp', 'dev')), may hold values from -6 to 6
- queries: bfloat16 [32768, 768], P(('grp', 'dev')), may hold values from -192 to 192
- token_rate: float32 [32768], P(('grp', 'dev')), may hold values from 0.00019934 to 0.00159472
- fast_weights: bfloat16 [3, 1536, 768], P(None, ('grp', 'dev')), may hold values from -0.21875 to 0.21875
Outputs:
- target_out: bfloat16 [32768, 768], P(('grp', 'dev'))
All inputs are finite; a program needn't handle non-finite values.
Results may differ from a plain program's by a relative error of at most 0.012.
The roundings to bfloat16 on the way count: a program that leaves them out, or rounds other values in their place, can miss the bound.
Values may be sent and summed in bfloat16 or wider, within the bound.
A program may use at most 64 MiB of HBM per device.

v0:
```python
import jax
import jax.numpy as jnp
from jax import lax
from jax.sharding import PartitionSpec as P

D = 768
HEADS = 12
HEAD_DIM = 64
epsilon = 1e-06


def rms_rows(matrix):
    return matrix / jnp.sqrt(jnp.mean(matrix * matrix, axis=-1, keepdims=True) + epsilon)


def gradient_rows(weights, key_normed, signal):
    gate_act = jnp.dot(key_normed, weights[0].T, preferred_element_type=jnp.float32)
    up_act = jnp.dot(key_normed, weights[1].T, preferred_element_type=jnp.float32)
    sigmoid_gate = jax.nn.sigmoid(gate_act)
    silu_gate = gate_act * sigmoid_gate
    hidden_bf = (silu_gate * up_act).astype(jnp.bfloat16)
    down_grad = jnp.dot(hidden_bf.T, signal, preferred_element_type=jnp.float32)
    hidden_grad = jnp.dot(signal, weights[2].T, preferred_element_type=jnp.float32)
    gate_grad = (
        hidden_grad * up_act * sigmoid_gate * (1.0 + gate_act * (1.0 - sigmoid_gate))
    ).astype(jnp.bfloat16)
    up_grad = (hidden_grad * silu_gate).astype(jnp.bfloat16)
    return jnp.stack(
        [
            jnp.dot(gate_grad.T, key_normed, preferred_element_type=jnp.float32),
            jnp.dot(up_grad.T, key_normed, preferred_element_type=jnp.float32),
            down_grad,
        ]
    )


def normalize_rows(old_bf, grad_rows):
    old_rows = old_bf.astype(jnp.float32)
    stepped = old_rows - grad_rows
    return (
        stepped
        * jnp.sqrt(jnp.mean(old_rows * old_rows, axis=-1, keepdims=True) + epsilon)
        / jnp.sqrt(jnp.mean(stepped * stepped, axis=-1, keepdims=True) + epsilon)
    ).astype(jnp.bfloat16)


def local_attention(query_block, key_block, value_block):
    query_count = query_block.shape[0]
    key_count = key_block.shape[0]
    query_heads = query_block.reshape(query_count, HEADS, HEAD_DIM)
    key_heads = key_block.reshape(key_count, HEADS, HEAD_DIM)
    value_heads = value_block.reshape(key_count, HEADS, HEAD_DIM)
    scores = jnp.einsum(
        "qhe,khe->hqk", query_heads, key_heads, preferred_element_type=jnp.float32
    ) * HEAD_DIM ** (-0.5)
    weights_bf = jax.nn.softmax(scores, axis=-1).astype(jnp.bfloat16)
    mixed = jnp.einsum("hqk,khe->qhe", weights_bf, value_heads, preferred_element_type=jnp.float32)
    return mixed.reshape(query_count, D)


def body(key_tokens, value_tokens, queries, token_rate, fast_weights):
    key_normed = rms_rows(key_tokens.astype(jnp.float32)).astype(jnp.bfloat16)
    signal = (-(token_rate[:, None] * value_tokens.astype(jnp.float32))).astype(jnp.bfloat16)
    all_keys, all_signals = (
        lax.all_gather(key_normed, "grp", axis=0, tiled=True),
        lax.all_gather(signal, "grp", axis=0, tiled=True),
    )
    attention_out = local_attention(queries, key_tokens, value_tokens)
    query_normed = rms_rows(queries.astype(jnp.float32)).astype(jnp.bfloat16)
    group_grad = gradient_rows(
        lax.all_gather(fast_weights, "dev", axis=1, tiled=True), all_keys, all_signals
    )
    owned_grad = lax.psum_scatter(group_grad, "dev", scatter_dimension=1, tiled=True)
    updated = normalize_rows(fast_weights, owned_grad)
    shard_rows = lax.all_gather(updated, ("grp", "dev"), axis=1, tiled=True)
    gate_act = jnp.dot(query_normed, shard_rows[0].T, preferred_element_type=jnp.float32)
    up_act = jnp.dot(query_normed, shard_rows[1].T, preferred_element_type=jnp.float32)
    hidden_bf = (jax.nn.silu(gate_act) * up_act).astype(jnp.bfloat16)
    fast_out = jnp.dot(hidden_bf, shard_rows[2], preferred_element_type=jnp.float32)
    return (fast_out + attention_out).astype(jnp.bfloat16)


def solution(mesh):
    in_specs = (
        P(("grp", "dev"), None),
        P(("grp", "dev"), None),
        P(("grp", "dev"), None),
        P(("grp", "dev")),
        P(None, ("grp", "dev"), None),
    )
    out_specs = P(("grp", "dev"), None)
    return jax.shard_map(body, mesh=mesh, in_specs=in_specs, out_specs=out_specs, check_vma=False)
```

profile of v0, /device:TPU:99, one launch (start us, length us, event | category | flops | bytes accessed | tf_op | source)
XLA Modules:
  0.0 1852.9 jit_solution(13766219696843032451)
XLA Ops:
  6.5 0.0 all-gather.3.cloned.1.call-start
  6.5 1.4 copy.23
  7.9 0.0 all-gather.3.cloned.1.call-update
  8.0 0.0 all-reduce.3.cloned.1.call-start
  8.0 1.0 fusion.19
  9.1 1.0 fusion.20
  10.1 1.0 negate_convert_fusion
  11.2 14.7 all_gather.14
  25.8 12.7 all_gather.12
  38.5 252.3 %all-gather.3.cloned.1.call-done = bf16[3,384,768]{2,0,1:T(4,128)(2,1)} async-done(((bf16[3,6,768]{2,0,1:T(4,128)(2,1)}), bf16[3,384,768]{2,0,1:T(4,128)(2,1)}) %all-gather.3.cloned.1.call-update) | async-done | bytes 1769488 | tf_op jit(solution)/shard_map/all_gather | solution.py:71
  290.9 6.5 fusion.37
  297.4 0.6 fusion.14
  298.0 0.6 fusion.15
  298.6 0.6 fusion.16
  299.2 0.6 convolution_bitcast_fusion.1
  299.8 0.7 convolution_bitcast_fusion.2
  300.5 0.6 convolution_bitcast_fusion
  301.1 2.0 pad_maximum_fusion
  303.1 0.0 copy-start.4
  303.1 0.0 copy-start.3
  303.1 0.0 copy-start
  303.1 0.0 copy-start.1
  303.1 0.0 copy-start.2
  303.1 0.0 all-reduce.3.cloned.1.call-update
  303.1 0.0 all-gather.5.cloned.1.call-start
  303.2 0.6 copy-done.4
  303.8 0.6 dynamic-slice
  305.0 713.5 %all-reduce.3.cloned.1.call-done = f32[3,384,768]{2,1,0:T(8,128)} async-done(((f32[3,384,768]{2,1,0:T(8,128)}), f32[3,384,768]{2,1,0:T(8,128)}) %all-reduce.3.cloned.1.call-update) | async-done | bytes 3538960
  1018.5 0.0 copy-done.3
  1018.5 1.0 fusion.26
  1019.5 1.0 divide_convert_fusion.2
  1020.5 0.6 copy.27
  1021.1 0.0 all-gather.5.cloned.1.call-update
  1021.2 0.0 copy-done
  1021.2 0.2 copy.32
  1021.3 0.0 copy-done.1
  1021.4 0.2 copy.33
  1021.5 0.0 copy-done.2
  1021.5 0.2 copy.31
  1021.7 0.4 fusion.38
  1022.1 0.3 convolution_multiply_fusion.1
  1022.5 0.3 fusion.23
  1022.8 0.2 copy.35
  1023.0 0.1 fusion.17
  1023.1 796.8 %all-gather.5.cloned.1.call-done = bf16[3,1536,768]{2,0,1:T(4,128)(2,1)} async-done(((bf16[3,6,768]{2,0,1:T(4,128)(2,1)}), bf16[3,1536,768]{2,0,1:T(4,128)(2,1)}) %all-gather.5.cloned.1.call-update) | async-done | bytes 7077904 | tf_op jit(solution)/shard_map/all_gather | solution.py:75
  1819.8 19.9 %fusion.36 = (bf16[1,1536,768]{2,0,1:T(2,128)(2,1)S(1)}, bf16[1,1536,768]{2,0,1:T(2,128)(2,1)}, bf16[1,1536,768]{2,0,1:T(2,128)(2,1)}) fusion(bf16[3,1536,768]{2,0,1:T(4,128)(2,1)} %all-gather.5.cloned.1.call-done), kind=kLoop, calls=%fused_computation.61 | loop fusion | bytes 14155776 | tf_op jit(solution)/shard_map/slice | solution.py:76
  1839.7 0.9 fusion.3
  1840.6 5.8 fusion.7
  (3 shorter events, 0.0 us)
Async XLA Ops:
  6.5 284.3 %all-gather.3.cloned.1.call-start = ((), (), s32[]{:S(2)}) async-start(), calls=%async_computation | async-start | bytes 2396160 | tf_op jit(solution)/shard_map/all_gather | solution.py:71
  8.0 1010.5 %all-reduce.3.cloned.1.call-start = ((), (), s32[]{:S(2)}) async-start(), calls=%async_computation.2 | async-start | bytes 7077888
  303.1 0.7 copy-start.4
  303.1 715.4 %copy-start.3 = (bf16[3,6,768]{2,1,0:T(8,128)(2,1)S(1)}, bf16[3,6,768]{2,1,0:T(8,128)(2,1)}, u32[]{:S(2)}) copy-start(bf16[3,6,768]{2,1,0:T(8,128)(2,1)} %param.9) | copy-start | bytes 82948
  303.1 718.1 %copy-start = (bf16[128,768]{1,0:T(8,128)(2,1)S(1)}, bf16[128,768]{1,0:T(8,128)(2,1)}, u32[]{:S(2)}) copy-start(bf16[128,768]{1,0:T(8,128)(2,1)} %param.5) | copy-start | bytes 589828
  303.1 718.2 %copy-start.1 = (bf16[128,768]{1,0:T(8,128)(2,1)S(1)}, bf16[128,768]{1,0:T(8,128)(2,1)}, u32[]{:S(2)}) copy-start(bf16[128,768]{1,0:T(8,128)(2,1)} %param.6) | copy-start | bytes 589828
  303.1 718.4 %copy-start.2 = (bf16[128,768]{1,0:T(8,128)(2,1)S(1)}, bf16[128,768]{1,0:T(8,128)(2,1)}, u32[]{:S(2)}) copy-start(bf16[128,768]{1,0:T(8,128)(2,1)} %param.7) | copy-start | bytes 589828
  303.1 1516.7 %all-gather.5.cloned.1.call-start = ((), (), s32[]{:S(2)}) async-start(), calls=%async_computation.1 | async-start | bytes 9474048 | tf_op jit(solution)/shard_map/all_gather | solution.py:75
Sparse Core Ops, SparseCore 0:
  9.1 281.6 all-gather.2
  303.3 715.1 all-reduce.2
  1021.3 798.5 all-gather.4
where the time goes:
time: 1850 us
  waiting for transfers between devices  1760 us (95%)
  local copies, waits for them, and re-layouts  30.2 us (2%)
  blocking collectives  27.4 us (1%)
    all_gather x1, waiting for transfers between devices, body(): shard_rows = lax.all_gather(updated, ('grp', 'dev'), axis=1, tiled=True)  797 us
    unnamed x4, waiting for transfers between devices  714 us
    all_gather x1, waiting for transfers between devices, body(): lax.all_gather(fast_weights, 'dev', axis=1, tiled=True)  252 us
  transfers between devices with their start and end apart: 3, of which 3 were waited for; matrix products, arithmetic and copies ran while one was open for 0% of the time, Pallas kernels for 0%

commit v1 on v0

--- a/solution.py
+++ b/solution.py
@@ -72,7 +72,10 @@
     )
     owned_grad = lax.psum_scatter(group_grad, "dev", scatter_dimension=1, tiled=True)
     updated = normalize_rows(fast_weights, owned_grad)
-    shard_rows = lax.all_gather(updated, ("grp", "dev"), axis=1, tiled=True)
+    shard_rows = jnp.concatenate(
+        lax.all_to_all(jnp.stack([updated] * lax.axis_size(("grp", "dev"))), ("grp", "dev"), 0, 0),
+        axis=1,
+    )
     gate_act = jnp.dot(query_normed, shard_rows[0].T, preferred_element_type=jnp.float32)
     up_act = jnp.dot(query_normed, shard_rows[1].T, preferred_element_type=jnp.float32)
     hidden_bf = (jax.nn.silu(gate_act) * up_act).astype(jnp.bfloat16)

time: 1850 us -> 1350 us (0.73)
  waiting for transfers between devices: 1760 us -> 1170 us
  starting transfers between devices: 0.09 us -> 84.5 us
    all_gather x1 -> x0, waiting for transfers between devices: 797 us -> none  [body(): shard_rows = lax.all_gather(updated, ('grp', 'dev'), axis=1, tiled=True)]
    all_to_all x0 -> x1, waiting for transfers between devices: none -> 203 us  [body(): lax.all_to_all(jnp.stack([updated] * lax.axis_size(('grp', 'dev'))), ('gr...]
    all_to_all x0 -> x1, starting transfers between devices: none -> 84.5 us  [body(): lax.all_to_all(jnp.stack([updated] * lax.axis_size(('grp', 'dev'))), ('gr...]
    unnamed x4 -> x3, waiting for transfers between devices: 714 us -> 713 us
where the time goes in v1:
time: 1350 us
  waiting for transfers between devices  1170 us (87%)
  starting transfers between devices  84.5 us (6%)
  local copies, waits for them, and re-layouts  33.3 us (2%)
  blocking collectives  27.4 us (2%)
  between operations  14.2 us (1%)
    unnamed x3, waiting for transfers between devices  713 us
    all_gather x1, waiting for transfers between devices, body(): lax.all_gather(fast_weights, 'dev', axis=1, tiled=True)  252 us
    all_to_all x1, waiting for transfers between devices, body(): lax.all_to_all(jnp.stack([updated] * lax.axis_size(('grp', 'dev'))), ('gr...  203 us
    all_to_all x1, starting transfers between devices, body(): lax.all_to_all(jnp.stack([updated] * lax.axis_size(('grp', 'dev'))), ('gr...  84.5 us
  transfers between devices with their start and end apart: 3, of which 3 were waited for; matrix products, arithmetic and copies ran while one was open for 0% of the time, Pallas kernels for 0%

profile of v1, /device:TPU:99, one launch (start us, length us, event | category | flops | bytes accessed | tf_op | source)
XLA Modules:
  0.0 1347.3 jit_solution(17051671591385286194)
XLA Ops:
  6.5 0.0 all-gather.2.cloned.1.call-start
  6.5 1.4 copy.22
  7.9 0.0 all-gather.2.cloned.1.call-update
  8.0 0.0 all-reduce.3.cloned.1.call-start
  8.0 1.0 fusion.18
  9.1 1.0 fusion.19
  10.1 1.0 negate_convert_fusion
  11.2 14.7 %all_gather.11 = bf16[512,768]{1,0:T(8,128)(2,1)S(1)} all-gather(bf16[128,768]{1,0:T(8,128)(2,1)S(1)} %fusion.19), channel_id=1, replica_groups=mesh['grp'=4,'dev'=64] {'grp'}, dimensions={0}, use_global_device_ids=true | all-gather | bytes 983040 | tf_op jit(solution)/shard_map/all_gather | solution.py:65
  25.8 12.7 all_gather.9
  38.5 252.3 %all-gather.2.cloned.1.call-done = bf16[3,384,768]{2,0,1:T(4,128)(2,1)} async-done(((bf16[3,6,768]{2,0,1:T(4,128)(2,1)}), bf16[3,384,768]{2,0,1:T(4,128)(2,1)}) %all-gather.2.cloned.1.call-update) | async-done | bytes 1769488 | tf_op jit(solution)/shard_map/all_gather | solution.py:71
  290.9 6.5 fusion.37
  297.4 0.6 fusion.13
  298.0 0.6 fusion.14
  298.6 0.6 fusion.15
  299.2 0.6 convolution_bitcast_fusion.1
  299.8 0.7 convolution_bitcast_fusion.2
  300.5 0.6 convolution_bitcast_fusion
  301.1 2.0 pad_maximum_fusion
  303.1 0.0 copy-start.6
  303.1 0.0 all-reduce.3.cloned.1.call-update
  303.1 0.6 copy-done.6
  303.8 0.6 dynamic-slice
  305.0 713.4 %all-reduce.3.cloned.1.call-done = f32[3,384,768]{2,1,0:T(8,128)} async-done(((f32[3,384,768]{2,1,0:T(8,128)}), f32[3,384,768]{2,1,0:T(8,128)}) %all-reduce.3.cloned.1.call-update) | async-done | bytes 3538960
  1018.5 0.0 copy-done.5
  1018.5 1.0 fusion.25
  1019.5 1.0 divide_convert_fusion.2
  1020.5 4.3 stack.14
  1024.8 84.5 %all-to-all-start = ((bf16[256,3,6,768]{3,2,1,0:T(8,128)(2,1)}), bf16[256,3,6,768]{3,2,1,0:T(8,128)(2,1)}, u32[]{:S(2)}, u32[]{:S(2)}) async-start(bf16[256,3,6,768]{3,2,1,0:T(8,128)(2,1)} %stack.14), calls=%async_computation | async-start | bytes 18874368 | tf_op jit(solution)/shard_map/all_to_all | solution.py:76
  1109.2 0.0 copy-done.1
  1109.2 0.2 copy.27
  1109.4 0.0 copy-done.2
  1109.4 0.2 copy.28
  1109.6 0.0 copy-done.3
  1109.6 0.2 copy.26
  1109.7 0.4 fusion.38
  1110.2 0.3 convolution_multiply_fusion.1
  1110.5 0.3 fusion.22
  1110.8 0.9 copy.30
  1111.8 0.1 fusion.16
  1111.9 202.6 %all-to-all-done = bf16[256,3,6,768]{3,2,1,0:T(8,128)(2,1)} async-done(((bf16[256,3,6,768]{3,2,1,0:T(8,128)(2,1)}), bf16[256,3,6,768]{3,2,1,0:T(8,128)(2,1)}, u32[]{:S(2)}, u32[]{:S(2)}) %all-to-all-start) | async-done | bytes 7077920 | tf_op jit(solution)/shard_map/all_to_all | solution.py:76
  1314.5 6.0 fusion.36
  1320.6 5.1 squeeze.21
  1325.7 5.1 squeeze.22
  1330.7 2.2 squeeze.23
  1333.0 3.6 fusion.34
  1336.6 0.0 copy-done
  1336.6 0.0 copy-done.4
  1336.6 3.9 fusion.6
  (9 shorter events, 0.0 us)
Async XLA Ops:
  6.5 284.3 %all-gather.2.cloned.1.call-start = ((), (), s32[]{:S(2)}) async-start(), calls=%async_computation.1 | async-start | bytes 2396160 | tf_op jit(solution)/shard_map/all_gather | solution.py:71
  8.0 1010.5 %all-reduce.3.cloned.1.call-start = ((), (), s32[]{:S(2)}) async-start(), calls=%async_computation.2 | async-start | bytes 7077888
  303.1 0.7 copy-start.6
  303.1 715.4 %copy-start.5 = (bf16[3,6,768]{2,1,0:T(8,128)(2,1)S(1)}, bf16[3,6,768]{2,1,0:T(8,128)(2,1)}, u32[]{:S(2)}) copy-start(bf16[3,6,768]{2,1,0:T(8,128)(2,1)} %param.9) | copy-start | bytes 82948
  1024.8 84.5 %copy-start.1 = (bf16[128,768]{1,0:T(8,128)(2,1)S(1)}, bf16[128,768]{1,0:T(8,128)(2,1)}, u32[]{:S(2)}) copy-start(bf16[128,768]{1,0:T(8,128)(2,1)} %param.5) | copy-start | bytes 589828
  1024.8 84.6 %copy-start.2 = (bf16[128,768]{1,0:T(8,128)(2,1)S(1)}, bf16[128,768]{1,0:T(8,128)(2,1)}, u32[]{:S(2)}) copy-start(bf16[128,768]{1,0:T(8,128)(2,1)} %param.6) | copy-start | bytes 589828
  1024.8 84.8 %copy-start.3 = (bf16[128,768]{1,0:T(8,128)(2,1)S(1)}, bf16[128,768]{1,0:T(8,128)(2,1)}, u32[]{:S(2)}) copy-start(bf16[128,768]{1,0:T(8,128)(2,1)} %param.7) | copy-start | bytes 589828
  1024.8 289.8 %all-to-all-start = ((bf16[256,3,6,768]{3,2,1,0:T(8,128)(2,1)}), bf16[256,3,6,768]{3,2,1,0:T(8,128)(2,1)}, u32[]{:S(2)}, u32[]{:S(2)}) async-start(bf16[256,3,6,768]{3,2,1,0:T(8,128)(2,1)} %stack.14), calls=%async_computation | async-start | bytes 18874368 | tf_op jit(solution)/shard_map/all_to_all | solution.py:76
  1333.0 3.6 copy-start
  1333.0 3.6 copy-start.4
Sparse Core Ops, SparseCore 0:
  9.1 281.6 all-gather.1
  303.2 715.1 all-reduce.2
